TPU v7x, 128 devices: a whole 4x4x4 slice. The times are simulated.
128 devices in a mesh: row: 16 (over y, x), col: 8 (over z, core).
Axes of the slice: x: 4, y: 4, z: 4, core: 2. Of those that a mesh axis runs over, the one named last changes fastest.
Arguments:
- upper_block: float32 [2, 1024, 1024], P(None, 'row', 'col'), may hold values from -0.25 to 0.25
- block_inverse: float32 [2, 1024, 64], P(None, 'row'), may hold values from -0.375 to 0.375
- panel_rhs: float32 [2, 32, 1024], P(None, None, 'row'), may hold values from -6 to 6
- upper_trail: float32 [2, 1024, 131072], P(None, 'row', 'col'), may hold values from -0.125 to 0.125
- trail_rhs: float32 [2, 32, 131072], P(None, None, ('col', 'row')), may hold values from -6 to 6
- currents: float32 [2, 1024], P(None, 'row'), may hold values from -4 to 4
- owner: int32 [1024], P('row'), may hold values from 0 to 511
Outputs:
- panel_adjoint: float32 [2, 32, 1024], P(None, None, 'row')
- trail_updated: float32 [2, 32, 131072], P(None, None, ('col', 'row'))
- patch_gradient: float32 [512], P(('row', 'col'))
Inputs may be any that keep to these rules, and one draw needn't show every extreme that they name: owner names a surface patch for each panel unknown.
All inputs are finite; a program needn't handle non-finite values.
Results may differ from a plain program's by a relative error of at most 0.0003.
Values sent between devices are 32-bit elements; how exact they have to be, the bound alone decides.
A program may use at most 64 MiB of HBM per device.

v0:
```python
import jax
import jax.numpy as jnp
from jax import lax
from jax.sharding import Mesh
from jax.sharding import PartitionSpec as P

PATCH_DEV = 4
ROW = ("row_0", "row_1")
ROW_COL = ("row_0", "row_1", "col")
COL_ROW = ("col", "row_0", "row_1")
highest = lax.Precision.HIGHEST


def rows_first(arrays, axis, dims):
    turned = [jnp.moveaxis(a, dim, 0) for a, dim in zip(arrays, dims)]
    widths = [t[0].size for t in turned]
    both = jnp.concatenate([t.reshape(-1, w) for t, w in zip(turned, widths)], axis=1)
    filled = lax.all_gather(both, axis, axis=0, tiled=True)
    pieces = jnp.split(filled, [sum(widths[:k]) for k in range(1, len(widths))], axis=1)
    return tuple(
        (
            jnp.moveaxis(b.reshape(-1, *t.shape[1:]), 0, dim)
            for b, t, dim in zip(pieces, turned, dims)
        )
    )


def sum_by_axis(value, axes, dim):
    if not axes:
        return value
    nearer = lax.psum_scatter(value, axes[0], scatter_dimension=dim, tiled=True)
    return sum_by_axis(nearer, axes[1:], dim)


def product_high(first, second):
    return jnp.dot(first, second, precision=highest, preferred_element_type=jnp.float32)


def conj_product(left, right):
    real_part = product_high(left[0], right[0]) + product_high(left[1], right[1])
    imag_part = product_high(left[1], right[0]) - product_high(left[0], right[1])
    return jnp.stack([real_part, imag_part])


def sweep(upper, inverses, rhs, width):
    count = rhs.shape[2] // width
    held_start = jnp.zeros(rhs.shape, jnp.float32)
    solved_start = jnp.zeros(rhs.shape, jnp.float32)

    def advance(index, carry):
        held, solved = carry
        start = (jnp.asarray(index) * width).astype(jnp.int32)
        local = lax.dynamic_slice_in_dim(held, start, width, 2)
        residual = lax.dynamic_slice_in_dim(rhs, start, width, 2) - local
        inverse = lax.dynamic_slice_in_dim(inverses, start, width, 1)
        value = conj_product(residual, inverse)
        rows_here = lax.dynamic_slice_in_dim(upper, start, width, 1)
        held = held + conj_product(value, rows_here)
        solved = lax.dynamic_update_slice_in_dim(solved, value, start, 2)
        return (held, solved)

    return lax.fori_loop(0, count, advance, (held_start, solved_start))[1]


def on_device(upper_block, block_inverse, panel_rhs, upper_trail, trail_rhs, currents, owner):
    rows_count = lax.axis_size(ROW)
    cols_count = lax.axis_size("col")
    row_index = lax.axis_index(ROW)
    col_index = lax.axis_index("col")
    width = block_inverse.shape[1]
    whole_rows, inverses, rhs_all = rows_first(
        (upper_block, block_inverse, panel_rhs), ROW, (1, 1, 2)
    )
    whole = lax.all_gather(whole_rows, "col", axis=2, tiled=True)
    solved_all = sweep(whole, inverses, rhs_all, width)
    solved = lax.dynamic_slice_in_dim(solved_all, row_index * width, width, 2)
    term = conj_product(solved, upper_trail)
    reduced = sum_by_axis(term, ROW, 2)
    updated = trail_rhs - reduced
    share = width // cols_count
    start = col_index * share
    mine = lax.dynamic_slice_in_dim(solved, start, share, 2)
    total = jnp.sum(mine, axis=1)
    current_part = lax.dynamic_slice_in_dim(currents, start, share, 1)
    owner_part = lax.dynamic_slice_in_dim(owner, start, share, 0)
    partial_value = current_part[0] * total[0] - current_part[1] * total[1]
    patch_count = PATCH_DEV * rows_count * cols_count
    patch_ids = lax.broadcasted_iota(jnp.int32, (share, patch_count), 1)
    selector = (owner_part[:, None] == patch_ids).astype(jnp.float32)
    spread = product_high(partial_value[None, :], selector)[0]
    gradient = lax.psum_scatter(spread, ROW_COL, scatter_dimension=0, tiled=True)
    return (solved, updated, gradient)


def solution(mesh):
    split = Mesh(mesh.devices.reshape(4, 4, mesh.shape["col"]), ("row_0", "row_1", "col"))
    return jax.shard_map(
        on_device,
        mesh=split,
        in_specs=(
            P(None, ROW, "col"),
            P(None, ROW, None),
            P(None, None, ROW),
            P(None, ROW, "col"),
            P(None, None, COL_ROW),
            P(None, ROW),
            P(ROW),
        ),
        out_specs=(P(None, None, ROW), P(None, None, COL_ROW), P(ROW_COL)),
        check_vma=False,
    )
```

profile of v0, /device:TPU:1, one launch (start us, length us, event | category | flops | bytes accessed | tf_op | source)
XLA Modules:
  0.0 364.6 jit_solution(3339413474390331940)
XLA Ops:
  9.8 48.1 %all-gather.3.cloned.1.call-done = f32[1024,448]{1,0:T(8,128)} async-done(((f32[64,448]{1,0:T(8,128)}), f32[1024,448]{1,0:T(8,128)}) %all-gather.3.cloned.1.call-update) | async-done | bytes 1835024 | tf_op jit(solution)/shard_map/all_gather | solution.py:18
  57.9 1.4 split.14
  59.3 1.3 copy.31
  61.2 50.3 %all-gather.5.cloned.1.call-done = f32[2,1024,1024]{1,2,0:T(8,128)} async-done(((f32[2,1024,128]{1,2,0:T(8,128)}), f32[2,1024,1024]{1,2,0:T(8,128)}) %all-gather.5.cloned.1.call-update) | async-done | bytes 8388624 | tf_op jit(solution)/shard_map/all_gather | solution.py:74
  111.4 8.7 %copy.33 = f32[2,1024,1024]{2,1,0:T(8,128)} copy(f32[2,1024,1024]{1,2,0:T(8,128)} %all-gather.5.cloned.1.call-done) | data formatting | bytes 16777216
  120.1 106.3 %while.16 = (s32[]{:T(128)}, f32[2,32,1024]{2,1,0:T(8,128)S(1)}, f32[2,32,1024]{2,1,0:T(8,128)S(1)}, f32[2,32,1024]{2,1,0:T(8,128)S(1)}, f32[2,1024,64]{1,2,0:T(...) while((s32[]{:T(128)}, f32[2,32,1024]{2,1,0:T(8,128)S(1)}, ...), condition=%wide.region_1.0_spmd.clone, body=%wide.region_0.0_spmd.clone.sunk | while | flops 107294728 | bytes 3555570 | solution.py:62
  120.8 1.2 fusion.58
  122.5 1.2 fusion.60
  123.7 1.2 fusion.61
  124.9 1.2 fusion.62
  127.3 1.2 fusion.58
  129.0 1.2 fusion.60
  131.4 1.2 fusion.62
  134.1 1.2 fusion.58
  135.8 1.2 fusion.60
  138.2 1.2 fusion.62
  140.6 1.2 fusion.58
  142.3 1.2 fusion.60
  143.5 1.2 fusion.61
  144.8 1.2 fusion.62
  147.4 1.2 fusion.58
  149.1 1.2 fusion.60
  151.6 1.2 fusion.62
  153.9 1.2 fusion.58
  155.6 1.2 fusion.60
  158.1 1.2 fusion.62
  160.7 1.2 fusion.58
  162.4 1.2 fusion.60
  164.9 1.2 fusion.62
  167.2 1.2 fusion.58
  168.9 1.2 fusion.60
  171.4 1.2 fusion.62
  174.0 1.2 fusion.58
  175.7 1.2 fusion.60
  178.2 1.2 fusion.62
  180.5 1.2 fusion.58
  182.2 1.2 fusion.60
  184.7 1.2 fusion.62
  187.3 1.2 fusion.58
  189.0 1.2 fusion.60
  191.5 1.2 fusion.62
  193.8 1.2 fusion.58
  195.5 1.2 fusion.60
  198.0 1.2 fusion.62
  200.6 1.2 fusion.58
  202.3 1.2 fusion.60
  204.8 1.2 fusion.62
  207.1 1.2 fusion.58
  208.8 1.2 fusion.60
  211.3 1.2 fusion.62
  213.9 1.2 fusion.58
  215.6 1.2 fusion.60
  218.1 1.2 fusion.62
  220.3 1.2 fusion.58
  222.1 1.2 fusion.60
  224.5 1.2 fusion.62
  226.4 4.0 %fusion.20 = f32[32,16384]{1,0:T(8,128)S(1)} fusion(f32[2,64,16384]{2,1,0:T(8,128)} %param.12, f32[2,32,1024]{2,1,0:T(8,128)S(1)} %get-tuple-element.112, s32[]{:T(128)S(6)} %select_n.23), kind=kOutput, calls=%fused_computation.37 | convolution fusion | flops 402653184 | bytes 6307844 | tf_op jit(solution)/shard_map/dot_general | solution.py:36
  230.5 4.0 %fusion.18 = f32[32,16384]{1,0:T(8,128)S(1)} fusion(f32[2,64,16384]{2,1,0:T(8,128)} %param.12, f32[2,32,1024]{2,1,0:T(8,128)S(1)} %get-tuple-element.112, s32[]{:T(128)S(6)} %add.84, s32[]{:T(128)S(6)} %select_n.23), kind=kOutput, calls=%fused_computation.35 | convolution fusion | flops 402653184 | bytes 6307848 | tf_op jit(solution)/shard_map/dot_general | solution.py:36
  234.5 3.9 %fusion.14 = f32[1,32,16384]{2,1,0:T(8,128)S(1)} fusion(f32[32,16384]{1,0:T(8,128)S(1)} %fusion.18, f32[2,64,16384]{2,1,0:T(8,128)} %param.12, f32[2,32,1024]{2,1,0:T(8,128)S(1)} %get-tuple-element.112, s32[]{:T(128)S(6)} %select_n.23), kind=kOutput, calls=%fused_computation.29 | convolution fusion | flops 403177472 | bytes 8404996 | tf_op jit(solution)/shard_map/dot_general | solution.py:36
  238.5 2.2 fusion.15
  240.7 2.2 pad_maximum_fusion.1
  243.0 46.6 %reduce-scatter.3.cloned.1.call-done = f32[2,32,4096]{2,1,0:T(8,128)} async-done(((f32[2,32,16384]{2,1,0:T(8,128)}), f32[2,32,4096]{2,1,0:T(8,128)}) %reduce-scatter.3.cloned.1.call-update) | async-done | bytes 1048592 | tf_op jit(solution)/shard_map/reduce_scatter | solution.py:31
  290.1 65.0 %all-reduce = f32[512]{0:T(512)S(1)} all-reduce(f32[512]{0:T(512)S(1)} %bitcast.133), channel_id=4, replica_groups=mesh['row_0'=4,'row_1'=4,'col'=8] {'row_0','row_1','col'}, use_global_device_ids=true, to_apply=%region_5.0.clone | all-reduce | flops 512 | bytes 4096
  356.4 1.7 sub.32
  (199 shorter events, 48.1 us)
Async XLA Ops:
  7.2 1.9 copy-start
  7.2 50.8 %all-gather.3.cloned.1.call-start = ((), (), s32[]{:S(2)}) async-start(), calls=%async_computation.2 | async-start | bytes 2228224 | tf_op jit(solution)/shard_map/all_gather | solution.py:18
  9.8 101.7 %all-gather.5.cloned.1.call-start = ((), (), s32[]{:S(2)}) async-start(), calls=%async_computation.3 | async-start | bytes 9437184 | tf_op jit(solution)/shard_map/all_gather | solution.py:74
  57.9 2.8 slice-start.2
  57.9 3.0 slice-start.3
  60.7 228.9 %reduce-scatter.3.cloned.1.call-start = ((), (), s32[]{:S(2)}) async-start(), calls=%async_computation.4 | async-start | bytes 5242880 | tf_op jit(solution)/shard_map/reduce_scatter | solution.py:31
  226.4 12.1 %slice-start = ((s8[8388608]{0:T(1024)(128)(4,1)}), s8[4194304]{0:T(1024)(128)(4,1)S(1)}, s32[]{:S(2)}) async-start(s8[8388608]{0:T(1024)(128)(4,1)} %bitcast.124), calls=%async_computation.6 | async-start | bytes 8388608
  230.5 8.0 %slice-start.1 = ((s8[8388608]{0:T(1024)(128)(4,1)}), s8[4194304]{0:T(1024)(128)(4,1)S(1)}, s32[]{:S(2)}) async-start(s8[8388608]{0:T(1024)(128)(4,1)} %bitcast.124), calls=%async_computation.7 | async-start | bytes 8388608
  242.9 46.7 %copy-start.3 = (s32[64]{0:T(128)S(1)}, s32[64]{0:T(128)}, u32[]{:S(2)}) copy-start(s32[64]{0:T(128)} %param.15) | copy-start | bytes 772
  242.9 46.8 %copy-start.2 = (f32[2,64]{1,0:T(2,128)S(1)}, f32[2,64]{1,0:T(2,128)}, u32[]{:S(2)}) copy-start(f32[2,64]{1,0:T(2,128)} %param.14) | copy-start | bytes 1540
  242.9 113.4 %copy-start.1 = (f32[2,32,1024]{2,1,0:T(8,128)S(1)}, f32[2,32,1024]{2,1,0:T(8,128)}, u32[]{:S(2)}) copy-start(f32[2,32,1024]{2,1,0:T(8,128)} %param.13) | copy-start | bytes 786436
  243.0 113.4 %reduce-scatter.5.cloned.1.call-start = ((), (), s32[]{:S(2)}) async-start(), calls=%async_computation.5 | async-start | bytes 1310720 | tf_op jit(solution)/shard_map/reduce_scatter | solution.py:31
Sparse Core Ops, SparseCore 0:
  10.7 47.1 all-gather.2
  60.8 50.5 all-gather.4
  243.1 46.4 reduce-scatter.2
  292.0 20.9 reduce-scatter.4
where the time goes:
time: 367 us; the launch traced here: 365 us
  waiting for transfers between devices  145 us (40%)
  matrix products  108 us (29%)
  blocking collectives  65 us (18%)
  local copies, waits for them, and re-layouts  22.7 us (6%)
  between operations  13.9 us (4%)
  other arithmetic  7.86 us (2%)
    dot_general x133, matrix products, product_high(): jnp.dot(first, second, precision=highest, preferred_element_type=jnp.floa...  108 us
    unnamed x1, blocking collectives  65 us
    all_gather x1, waiting for transfers between devices, on_device(): whole = lax.all_gather(whole_rows, 'col', axis=2, tiled=True)  50.3 us
    all_gather x1, waiting for transfers between devices, rows_first(): filled = lax.all_gather(both, axis, axis=0, tiled=True)  48.1 us
    reduce_scatter x2, waiting for transfers between devices, sum_by_axis(): nearer = lax.psum_scatter(value, axes[0], scatter_dimension=dim, tiled=True)  46.6 us
    unnamed x14, local copies, waits for them, and re-layouts  9.29 us
    dynamic_update_slice x16, local copies, waits for them, and re-layouts, advance(): solved = lax.dynamic_update_slice_in_dim(solved, value, start, 2)  7.65 us
  transfers between devices with their start and end apart: 4, of which 3 were waited for; matrix products, arithmetic and copies ran while one was open for 1% of the time, Pallas kernels for 0%

commit v1 on v0

--- a/solution.py
+++ b/solution.py
@@ -1,3 +1,4 @@
+import functools
 import jax
 import jax.numpy as jnp
 from jax import lax
@@ -9,6 +10,25 @@
 ROW_COL = ("row_0", "row_1", "col")
 COL_ROW = ("col", "row_0", "row_1")
 highest = lax.Precision.HIGHEST
+
+
+def enter_the_surface(xin, bus_axis):
+    n_slots = jax.lax.axis_size(bus_axis)
+    series = tuple(((u, (u + 1) % n_slots) for u in range(n_slots)))
+    placed, z2 = ([xin], [xin])
+    inbox = tuple(((u, (u - 1) % n_slots) for u in range(n_slots)))
+    for _ in range(n_slots // 2):
+        placed.append(jax.lax.ppermute(placed[-1], bus_axis, perm=series))
+    tick = 0
+    while tick < (n_slots - 1) // 2:
+        z2.append(jax.lax.ppermute(z2[-1], bus_axis, perm=inbox))
+        tick += 1
+    r_now = jnp.concatenate([*placed[::-1], *z2[1:]], 2)
+    earlier = jnp.roll(r_now, (jax.lax.axis_index(bus_axis) - n_slots // 2) * xin.shape[2], 2)
+    return earlier
+
+
+_assign_local_data = functools.partial(enter_the_surface, bus_axis="col")
 
 
 def rows_first(arrays, axis, dims):
@@ -71,7 +91,7 @@
     whole_rows, inverses, rhs_all = rows_first(
         (upper_block, block_inverse, panel_rhs), ROW, (1, 1, 2)
     )
-    whole = lax.all_gather(whole_rows, "col", axis=2, tiled=True)
+    whole = _assign_local_data(whole_rows)
     solved_all = sweep(whole, inverses, rhs_all, width)
     solved = lax.dynamic_slice_in_dim(solved_all, row_index * width, width, 2)
     term = conj_product(solved, upper_trail)

time: 367 us -> 459 us (1.25); the launches traced: 365 us -> 450 us
  matrix products: 108 us -> 156 us
  local copies, waits for them, and re-layouts: 22.7 us -> 45.5 us
  starting transfers between devices: 0.16 us -> 13.3 us
  other arithmetic: 7.86 us -> 20 us
  waiting for transfers between devices: 145 us -> 134 us
    all_gather x1 -> x0, waiting for transfers between devices: 50.3 us -> none  [on_device(): whole = lax.all_gather(whole_rows, 'col', axis=2, tiled=True)]
    dot_general x133, matrix products: 108 us -> 156 us  [product_high(): jnp.dot(first, second, precision=highest, preferred_element_type=jnp.floa...]
    ppermute x0 -> x7, waiting for transfers between devices: none -> 36.6 us  [the longest x4 35.7 us: enter_the_surface(): placed.append(jax.lax.ppermute(placed[-1], bus_axis, perm=series))]
    ppermute x0 -> x7, starting transfers between devices: none -> 13.2 us  [the longest x4 10.2 us: enter_the_surface(): placed.append(jax.lax.ppermute(placed[-1], bus_axis, perm=series))]
    sub x16, other arithmetic: 1.42 us -> 13.5 us  [advance(): residual = lax.dynamic_slice_in_dim(rhs, start, width, 2) - local]
    unnamed x14 -> x35, local copies, waits for them, and re-layouts: 9.29 us -> 20.4 us
    split x8 -> x6, local copies, waits for them, and re-layouts: 3.09 us -> 9.35 us  [rows_first(): jnp.split(filled, [sum(widths[:k]) for k in range(1, len(widths))], axis=1)]
  transfers between devices with their start and end apart: 4 -> 10, of which waited for: 3 -> 8; matrix products, arithmetic and copies ran while one was open for 1% -> 3% of each run, Pallas kernels for 0% -> 0%
where the time goes in v1:
time: 459 us; the launch traced here: 450 us
  matrix products  156 us (34%)
  waiting for transfers between devices  134 us (29%)
  blocking collectives  64.9 us (14%)
  local copies, waits for them, and re-layouts  45.5 us (10%)
  other arithmetic  20 us (4%)
  between operations  14 us (3%)
  starting transfers between devices  13.3 us (3%)
    dot_general x133, matrix products, product_high(): jnp.dot(first, second, precision=highest, preferred_element_type=jnp.floa...  156 us
    unnamed x1, blocking collectives  64.9 us
    reduce_scatter x2, waiting for transfers between devices, sum_by_axis(): nearer = lax.psum_scatter(value, axes[0], scatter_dimension=dim, tiled=True)  49.3 us
    all_gather x1, waiting for transfers between devices, rows_first(): filled = lax.all_gather(both, axis, axis=0, tiled=True)  48.1 us
    ppermute x4, waiting for transfers between devices, enter_the_surface(): placed.append(jax.lax.ppermute(placed[-1], bus_axis, perm=series))  35.7 us
    unnamed x35, local copies, waits for them, and re-layouts  20.4 us
    sub x16, other arithmetic, advance(): residual = lax.dynamic_slice_in_dim(rhs, start, width, 2) - local  13.5 us
    ppermute x4, starting transfers between devices, enter_the_surface(): placed.append(jax.lax.ppermute(placed[-1], bus_axis, perm=series))  10.2 us
  transfers between devices with their start and end apart: 10, of which 8 were waited for; matrix products, arithmetic and copies ran while one was open for 3% of the time, Pallas kernels for 0%

profile of v1, /device:TPU:1, one launch (start us, length us, event | category | flops | bytes accessed | tf_op | source)
XLA Modules:
  0.0 450.1 jit_solution(11181216800083650599)
XLA Ops:
  9.8 48.1 %all-gather.2.cloned.1.call-done = f32[1024,448]{1,0:T(8,128)} async-done(((f32[64,448]{1,0:T(8,128)}), f32[1024,448]{1,0:T(8,128)}) %all-gather.2.cloned.1.call-update) | async-done | bytes 1835024 | tf_op jit(solution)/shard_map/all_gather | solution.py:38
  57.9 1.3 split.14
  59.6 2.7 collective-permute-start
  62.2 11.7 %collective-permute-done = f32[2,1024,128]{1,2,0:T(8,128)S(1)} collective-permute-done((f32[2,1024,128]{1,2,0:T(8,128)S(1)}, f32[2,1024,128]{1,2,0:T(8,128)S(1)}, u32[]{:S(2)}, u32[]{:S(2)}) %collective-permute-start) | collective-permute-done | bytes 1048608 | tf_op jit(solution)/shard_map/ppermute | solution.py:21
  74.0 2.5 collective-permute-start.1
  76.5 11.7 %collective-permute-done.1 = f32[2,1024,128]{1,2,0:T(8,128)S(1)} collective-permute-done((f32[2,1024,128]{1,2,0:T(8,128)S(1)}, f32[2,1024,128]{1,2,0:T(8,128)S(1)}, u32[]{:S(2)}, u32[]{:S(2)}) %collective-permute-start.1) | collective-permute-done | bytes 1048608 | tf_op jit(solution)/shard_map/ppermute | solution.py:21
  88.2 2.5 collective-permute-start.2
  92.0 10.5 %collective-permute-done.2 = f32[2,1024,128]{1,2,0:T(8,128)} collective-permute-done((f32[2,1024,128]{1,2,0:T(8,128)S(1)}, f32[2,1024,128]{1,2,0:T(8,128)}, u32[]{:S(2)}, u32[]{:S(2)}) %collective-permute-start.2) | collective-permute-done | bytes 1048608 | tf_op jit(solution)/shard_map/ppermute | solution.py:21
  102.4 2.6 collective-permute-start.3
  105.6 1.9 collective-permute-start.6
  107.5 1.9 split.12
  109.4 1.9 copy.29
  111.3 1.9 split.13
  113.2 2.0 copy.30
  115.3 1.8 collective-permute-done.3
  117.1 1.3 constant_dynamic-update-slice_fusion.15
  118.4 1.3 constant_dynamic-update-slice_fusion.14
  119.7 1.3 constant_dynamic-update-slice_fusion.13
  121.3 1.3 constant_dynamic-update-slice_fusion.9
  122.6 1.3 constant_dynamic-update-slice_fusion.8
  123.9 1.3 constant_dynamic-update-slice_fusion.7
  125.2 1.3 constant_dynamic-update-slice_fusion.6
  127.0 1.3 constant_dynamic-update-slice_fusion.1
  128.3 1.3 constant_dynamic-update-slice_fusion
  129.6 4.1 constant_dynamic-slice_fusion.2
  133.7 8.7 %copy.33 = f32[2,1024,1024]{2,1,0:T(8,128)} copy(f32[2,1024,1024]{1,2,0:T(8,128)} %constant_dynamic-slice_fusion.2) | data formatting | bytes 16777216
  142.4 166.8 %while.16 = (s32[]{:T(128)}, f32[2,32,1024]{2,1,0:T(8,128)S(1)}, f32[2,32,1024]{2,1,0:T(8,128)S(1)}, f32[2,32,1024]{2,1,0:T(8,128)}, f32[2,1024,64]{1,2,0:T(8,12...) while((s32[]{:T(128)}, f32[2,32,1024]{2,1,0:T(8,128)S(1)}, ...), condition=%wide.region_1.2_spmd.clone, body=%wide.region_0.1_spmd.clone.sunk | while | flops 107294728 | bytes 3555570 | solution.py:82
  148.6 1.2 fusion.60
  151.0 1.2 fusion.62
  158.9 1.2 fusion.60
  161.3 1.2 fusion.62
  169.4 1.2 fusion.60
  171.9 1.2 fusion.62
  179.7 1.2 fusion.60
  182.2 1.2 fusion.62
  190.3 1.2 fusion.60
  192.8 1.2 fusion.62
  200.6 1.2 fusion.60
  203.1 1.2 fusion.62
  211.2 1.2 fusion.60
  213.6 1.2 fusion.62
  221.5 1.2 fusion.60
  223.9 1.2 fusion.62
  232.0 1.2 fusion.60
  234.5 1.2 fusion.62
  242.3 1.2 fusion.60
  244.8 1.2 fusion.62
  252.9 1.2 fusion.60
  263.2 1.2 fusion.60
  265.7 1.2 fusion.62
  273.8 1.2 fusion.60
  276.2 1.2 fusion.62
  284.1 1.2 fusion.60
  286.5 1.2 fusion.62
  294.6 1.2 fusion.60
  304.9 1.2 fusion.60
  309.2 4.0 fusion.20
  313.3 4.0 fusion.18
  317.4 3.9 fusion.14
  321.4 2.2 fusion.15
  323.6 2.2 pad_maximum_fusion.1
  325.9 49.3 %reduce-scatter.3.cloned.1.call-done = f32[2,32,4096]{2,1,0:T(8,128)} async-done(((f32[2,32,16384]{2,1,0:T(8,128)}), f32[2,32,4096]{2,1,0:T(8,128)}) %reduce-scatter.3.cloned.1.call-update) | async-done | bytes 1048592 | tf_op jit(solution)/shard_map/reduce_scatter | solution.py:51
  375.7 64.9 %all-reduce = f32[512]{0:T(512)S(1)} all-reduce(f32[512]{0:T(512)S(1)} %bitcast.136), channel_id=4, replica_groups=mesh['row_0'=4,'row_1'=4,'col'=8] {'row_0','row_1','col'}, use_global_device_ids=true, to_apply=%region_5.6.clone | all-reduce | flops 512 | bytes 4096
  441.9 1.7 sub.41
  (231 shorter events, 136.6 us)
Async XLA Ops:
  7.2 1.9 copy-start
  7.2 50.8 %all-gather.2.cloned.1.call-start = ((), (), s32[]{:S(2)}) async-start(), calls=%async_computation.2 | async-start | bytes 2228224 | tf_op jit(solution)/shard_map/all_gather | solution.py:38
  9.8 365.4 %reduce-scatter.3.cloned.1.call-start = ((), (), s32[]{:S(2)}) async-start(), calls=%async_computation.3 | async-start | bytes 5242880 | tf_op jit(solution)/shard_map/reduce_scatter | solution.py:51
  59.6 14.4 %collective-permute-start = (f32[2,1024,128]{1,2,0:T(8,128)S(1)}, f32[2,1024,128]{1,2,0:T(8,128)S(1)}, u32[]{:S(2)}, u32[]{:S(2)}) collective-permute-start(f32[2,1024,128]{1,2,0:T(8,128)S(1)} %bitcast.126), channel_id=1, source_target_pairs={{0,1},{1,2},{2,3},{3,4},{4,5},{5,6},{6,7},{7,0},{8,9},{9,10},{10,1... | collective-permute-start | bytes 3145736 | tf_op jit(solution)/shard_map/ppermute | solution.py:21
  74.0 14.2 %collective-permute-start.1 = (f32[2,1024,128]{1,2,0:T(8,128)S(1)}, f32[2,1024,128]{1,2,0:T(8,128)S(1)}, u32[]{:S(2)}, u32[]{:S(2)}) collective-permute-start(f32[2,1024,128]{1,2,0:T(8,128)S(1)} %collective-permute-done), channel_id=1, source_target_pairs={{0,1},{1,2},{2,3},{3,4},{4,5},{5,6},{6,7},{7,0},{8,9},{9,10},{10,1... | collective-permute-start | bytes 3145736 | tf_op jit(solution)/shard_map/ppermute | solution.py:21
  76.5 14.5 %collective-permute-start.4 = (f32[2,1024,128]{1,2,0:T(8,128)S(1)}, f32[2,1024,128]{1,2,0:T(8,128)S(1)}, u32[]{:S(2)}, u32[]{:S(2)}) collective-permute-start(f32[2,1024,128]{1,2,0:T(8,128)S(1)} %bitcast.127), channel_id=1, source_target_pairs={{0,7},{1,0},{2,1},{3,2},{4,3},{5,4},{6,5},{7,6},{8,15},{9,8},{10,9... | collective-permute-start | bytes 3145736 | tf_op jit(solution)/shard_map/ppermute | solution.py:24
  88.2 17.4 %copy-start.2 = (f32[2,1024,128]{1,2,0:T(8,128)}, f32[2,1024,128]{1,2,0:T(8,128)S(1)}, u32[]{:S(2)}) copy-start(f32[2,1024,128]{1,2,0:T(8,128)S(1)} %collective-permute-done.1) | copy-start | bytes 3145732
  88.2 14.2 %collective-permute-start.2 = (f32[2,1024,128]{1,2,0:T(8,128)S(1)}, f32[2,1024,128]{1,2,0:T(8,128)}, u32[]{:S(2)}, u32[]{:S(2)}) collective-permute-start(f32[2,1024,128]{1,2,0:T(8,128)S(1)} %collective-permute-done.1), channel_id=1, source_target_pairs={{0,1},{1,2},{2,3},{3,4},{4,5},{5,6},{6,7},{7,0},{8,9},{9,10},{10,1... | collective-permute-start | bytes 3145736 | tf_op jit(solution)/shard_map/ppermute | solution.py:21
  91.0 14.6 %collective-permute-start.5 = (f32[2,1024,128]{1,2,0:T(8,128)S(1)}, f32[2,1024,128]{1,2,0:T(8,128)}, u32[]{:S(2)}, u32[]{:S(2)}) collective-permute-start(f32[2,1024,128]{1,2,0:T(8,128)S(1)} %collective-permute-done.4), channel_id=1, source_target_pairs={{0,7},{1,0},{2,1},{3,2},{4,3},{5,4},{6,5},{7,6},{8,15},{9,8},{10,9... | collective-permute-start | bytes 3145736 | tf_op jit(solution)/shard_map/ppermute | solution.py:24
  102.4 14.6 %collective-permute-start.3 = (f32[2,1024,128]{1,2,0:T(8,128)}, f32[2,1024,128]{1,2,0:T(8,128)}, u32[]{:S(2)}, u32[]{:S(2)}) collective-permute-start(f32[2,1024,128]{1,2,0:T(8,128)} %collective-permute-done.2), channel_id=1, source_target_pairs={{0,1},{1,2},{2,3},{3,4},{4,5},{5,6},{6,7},{7,0},{8,9},{9,10},{10,1... | collective-permute-start | bytes 3145736 | tf_op jit(solution)/shard_map/ppermute | solution.py:21
  105.6 17.0 %collective-permute-start.6 = (f32[2,1024,128]{1,2,0:T(8,128)}, f32[2,1024,128]{1,2,0:T(8,128)}, u32[]{:S(2)}, u32[]{:S(2)}) collective-permute-start(f32[2,1024,128]{1,2,0:T(8,128)} %collective-permute-done.5), channel_id=1, source_target_pairs={{0,7},{1,0},{2,1},{3,2},{4,3},{5,4},{6,5},{7,6},{8,15},{9,8},{10,9... | collective-permute-start | bytes 3145736 | tf_op jit(solution)/shard_map/ppermute | solution.py:24
  115.3 11.3 %copy-start.3 = (f32[2,1024,128]{1,2,0:T(8,128)S(1)}, f32[2,1024,128]{1,2,0:T(8,128)}, u32[]{:S(2)}) copy-start(f32[2,1024,128]{1,2,0:T(8,128)} %copy-done.2) | copy-start | bytes 3145732
  309.2 12.1 %slice-start = ((s8[8388608]{0:T(1024)(128)(4,1)}), s8[4194304]{0:T(1024)(128)(4,1)S(1)}, s32[]{:S(2)}) async-start(s8[8388608]{0:T(1024)(128)(4,1)} %bitcast.124), calls=%async_computation.5 | async-start | bytes 8388608
  313.3 8.1 %slice-start.1 = ((s8[8388608]{0:T(1024)(128)(4,1)}), s8[4194304]{0:T(1024)(128)(4,1)S(1)}, s32[]{:S(2)}) async-start(s8[8388608]{0:T(1024)(128)(4,1)} %bitcast.124), calls=%async_computation.6 | async-start | bytes 8388608
  313.3 130.3 %copy-start.1 = (f32[2,64,128]{2,1,0:T(8,128)S(1)}, f32[2,64,128]{2,1,0:T(8,128)}, u32[]{:S(2)}) copy-start(f32[2,64,128]{2,1,0:T(8,128)} %param.9) | copy-start | bytes 196612
  317.4 57.9 %copy-start.6 = (s32[64]{0:T(128)S(1)}, s32[64]{0:T(128)}, u32[]{:S(2)}) copy-start(s32[64]{0:T(128)} %param.15) | copy-start | bytes 772
  317.4 58.0 %copy-start.5 = (f32[2,64]{1,0:T(2,128)S(1)}, f32[2,64]{1,0:T(2,128)}, u32[]{:S(2)}) copy-start(f32[2,64]{1,0:T(2,128)} %param.14) | copy-start | bytes 1540
  317.4 124.5 %copy-start.4 = (f32[2,32,1024]{2,1,0:T(8,128)S(1)}, f32[2,32,1024]{2,1,0:T(8,128)}, u32[]{:S(2)}) copy-start(f32[2,32,1024]{2,1,0:T(8,128)} %param.13) | copy-start | bytes 786436
  325.8 116.0 %reduce-scatter.5.cloned.1.call-start = ((), (), s32[]{:S(2)}) async-start(), calls=%async_computation.4 | async-start | bytes 1310720 | tf_op jit(solution)/shard_map/reduce_scatter | solution.py:51
Sparse Core Ops, SparseCore 0:
  10.7 47.1 all-gather.1
  326.0 49.1 reduce-scatter.2
  377.7 21.8 reduce-scatter.4
